TPU v7x, 128 devices: a whole 4x4x4 slice. The times are simulated.
128 devices in a mesh: row: 16 (over y, z_lo, core), col: 8 (over z_hi, x).
Axes of the slice: x: 4, y: 4, z: 4 (z_hi: 2, z_lo: 2; z = z_hi * 2 + z_lo), core: 2. Of those that a mesh axis runs over, the one named last changes fastest.
Arguments:
- points: float32 [49152, 16], P(('row', 'col')), may hold values from -6 to 6
- targets: float32 [49152, 16], P(('row', 'col')), may hold values from -6 to 6
- initial: float32 [49152, 16], P(('row', 'col')), may hold values from -3 to 3
- lengthscale: float32 [16], replicated, may hold values from 2 to 8
Outputs:
- solution: float32 [49152, 16], P(('row', 'col'))
- residual: float32 [49152, 16], P(('row', 'col'))
All inputs are finite; a program needn't handle non-finite values.
Results may differ from a plain program's by a relative error of at most 0.0003.
Values sent between devices are 32-bit elements; how exact they have to be, the bound alone decides.
A program may use at most 64 MiB of HBM per device.

v0:
```python
import jax
import jax.numpy as jnp
from jax import lax
from jax.sharding import PartitionSpec as P

ITERS = 2


ROOT_FIVE = 5.0**0.5
NOISE_VAR = 0.5


def matern_kernel(left_pts, left_sq, right_pts, right_sq):
    crossed = jnp.dot(left_pts, right_pts.T, precision=lax.Precision.HIGHEST)
    squared = jnp.maximum(left_sq[:, None] + right_sq[None, :] - 2.0 * crossed, 0.0)
    distance = jnp.sqrt(squared)
    return (1.0 + ROOT_FIVE * distance + 5.0 / 3.0 * squared) * jnp.exp(-ROOT_FIVE * distance)


def matern_apply(left_pts, left_sq, right_pts, right_sq, vectors):
    kernel = matern_kernel(left_pts, left_sq, right_pts, right_sq)
    return jnp.dot(kernel, vectors, precision=lax.Precision.HIGHEST)


def pick_breadth(length, unit, left_rows):
    limit = max(unit, (1 << 22) // left_rows)
    breadth = unit
    while breadth * 2 <= limit and length % (breadth * 2) == 0:
        breadth = breadth * 2
    return breadth


def fold_blocks(running, left_pts, left_sq, right_pts, right_vecs, unit):
    length = right_pts.shape[0]
    breadth = pick_breadth(length, unit, left_pts.shape[0])
    turns = length // breadth
    pts_blocks = right_pts.reshape(turns, breadth, right_pts.shape[1])
    vec_blocks = right_vecs.reshape(turns, breadth, right_vecs.shape[1])

    def advance(carried, blocks):
        block_pts, block_vecs = blocks
        block_sq = jnp.sum(block_pts * block_pts, axis=1)
        return (carried + matern_apply(left_pts, left_sq, block_pts, block_sq, block_vecs), None)

    result, unused = lax.scan(advance, running, (pts_blocks, vec_blocks))
    return result


def col_sums(first, second):
    return jnp.sum(first * second, axis=0)


def residual_norm(current):
    return lax.psum(col_sums(current, current), ("row", "col"))


def shards(points, targets, initial, lengthscale):
    scaled = points / lengthscale[None, :]
    own_rows = scaled.shape[0]
    own_sq = jnp.sum(scaled * scaled, axis=1)
    all_pts = lax.all_gather(scaled, ("row", "col"), axis=0, tiled=True)

    def operate(vectors):
        empty = jnp.zeros(vectors.shape, jnp.float32)
        summed = fold_blocks(
            empty,
            scaled,
            own_sq,
            all_pts,
            lax.all_gather(vectors, ("row", "col"), axis=0, tiled=True),
            own_rows,
        )
        return summed + NOISE_VAR * vectors

    solution = initial
    residual = targets - operate(initial)
    direction = residual
    norm_now = residual_norm(residual)
    for number in range(ITERS):
        image = operate(direction)
        curve = lax.psum(col_sums(direction, image), ("row", "col"))
        step_size = norm_now / curve
        solution = solution + step_size[None, :] * direction
        residual = residual - step_size[None, :] * image
        norm_next = residual_norm(residual)
        direction = residual + (norm_next / norm_now)[None, :] * direction
        norm_now = norm_next
    return (solution, residual)


def solution(mesh):
    in_specs = (P(("row", "col"), None), P(("row", "col"), None), P(("row", "col"), None), P())
    out_specs = (P(("row", "col"), None), P(("row", "col"), None))
    return jax.shard_map(shards, mesh=mesh, in_specs=in_specs, out_specs=out_specs, check_vma=False)
```

profile of v0, /device:TPU:1, one launch (start us, length us, event | category | flops | bytes accessed | tf_op | source)
XLA Modules:
  0.0 1989.5 jit_solution(13966345082628248732)
XLA Ops:
  9.5 308.4 %all-gather.7.cloned.1.call-done = f32[49152,16]{0,1:T(8,128)} async-done(((f32[384,16]{0,1:T(8,128)}), f32[49152,16]{0,1:T(8,128)}) %all-gather.7.cloned.1.call-update) | async-done | bytes 3145744 | tf_op jit(solution)/shard_map/all_gather | solution.py:70
  323.2 302.0 %all-gather.5.cloned.1.call-done = f32[49152,16]{0,1:T(8,128)} async-done(((f32[384,16]{0,1:T(8,128)}), f32[49152,16]{0,1:T(8,128)}) %all-gather.5.cloned.1.call-update) | async-done | bytes 3145744 | tf_op jit(solution)/shard_map/all_gather | solution.py:61
  627.4 185.6 %while.33 = (s32[]{:T(128)}, f32[384,16]{0,1:T(8,128)S(1)}, f32[384]{0:T(512)S(1)}, f32[8,6144,16]{1,2,0:T(8,128)S(1)}, f32[384,16]{0,1:T(8,128)S(1)}, /*index=5*/f32[8,6144,16]{1,0,2:T(8,128)}, s32[]{:T(128)}, s32[]{:T(128)}) while((s32[]{:T(128)}, f32[384,16]{0,1:T(8,128)S(1)}, f32[384]{0:T(512)S(1)}, ...), condition=%wide.region_3.4_spmd.clone, body=%wide.region_1.3_spmd.clone.sunk | while | flops 929765376 | bytes 20964980 | solution.py:45
  652.8 10.8 fusion.131
  674.1 10.8 fusion.131
  695.5 10.8 fusion.131
  716.8 10.8 fusion.131
  738.2 10.8 fusion.131
  759.6 10.8 fusion.131
  780.9 10.8 fusion.131
  802.3 10.8 fusion.131
  813.8 305.2 %all-gather.9.cloned.1.call-done = f32[49152,16]{0,1:T(8,128)} async-done(((f32[384,16]{0,1:T(8,128)}), f32[49152,16]{0,1:T(8,128)}) %all-gather.9.cloned.1.call-update) | async-done | bytes 3145744 | tf_op jit(solution)/shard_map/all_gather | solution.py:70
  1124.4 184.4 %while.34 = (s32[]{:T(128)}, f32[384,16]{0,1:T(8,128)S(1)}, f32[384]{0:T(512)S(1)}, f32[8,6144,16]{1,2,0:T(8,128)S(1)}, f32[384,16]{0,1:T(8,128)S(1)}, /*index=5*/f32[8,6144,16]{1,0,2:T(8,128)}, s32[]{:T(128)}, s32[]{:T(128)}) while((s32[]{:T(128)}, f32[384,16]{0,1:T(8,128)S(1)}, f32[384]{0:T(512)S(1)}, ...), condition=%wide.region_8.9_spmd.clone, body=%wide.region_6.8_spmd.clone.sunk | while | flops 929765376 | bytes 20964980 | solution.py:45
  1148.1 10.8 fusion.137
  1169.5 10.8 fusion.137
  1190.8 10.8 fusion.137
  1212.2 10.8 fusion.137
  1233.5 10.8 fusion.137
  1254.9 10.8 fusion.137
  1276.2 10.8 fusion.137
  1297.6 10.8 fusion.137
  1308.9 65.4 %all-reduce = (f32[16]{0:T(128)S(1)}, f32[16]{0:T(128)S(1)}) all-reduce(f32[16]{0:T(128)S(1)} %get-tuple-element.195, f32[16]{0:T(128)S(1)} %get-tuple-element.194), channel_id=1, replica_groups=mesh['row'=16,'col'=8] {'row','col'}, use_global_device_ids=true, to_apply=%region_5.6 | all-reduce | flops 32 | bytes 256 | tf_op jit(solution)/shard_map/psum | solution.py:54
  1374.6 62.7 %psum.30 = f32[16]{0:T(128)S(1)} all-reduce(f32[16]{0:T(128)S(1)} %multiply_reduce_fusion.1), channel_id=1, replica_groups=mesh['row'=16,'col'=8] {'row','col'}, use_global_device_ids=true, to_apply=%region_12.13 | all-reduce | flops 16 | bytes 128 | tf_op jit(solution)/shard_map/psum | solution.py:54
  1438.0 302.2 %all-gather.11.cloned.1.call-done = f32[49152,16]{0,1:T(8,128)} async-done(((f32[384,16]{0,1:T(8,128)}), f32[49152,16]{0,1:T(8,128)}) %all-gather.11.cloned.1.call-update) | async-done | bytes 3145744 | tf_op jit(solution)/shard_map/all_gather | solution.py:70
  1745.6 170.9 %while.35 = (s32[]{:T(128)}, f32[384,16]{0,1:T(8,128)S(1)}, f32[384]{0:T(512)S(1)}, f32[8,6144,16]{1,2,0:T(8,128)S(1)}, f32[384,16]{0,1:T(8,128)S(1)}, /*index=5*/f32[8,6144,16]{1,0,2:T(8,128)}, s32[]{:T(128)}, s32[]{:T(128)}) while((s32[]{:T(128)}, f32[384,16]{0,1:T(8,128)S(1)}, f32[384]{0:T(512)S(1)}, ...), condition=%wide.region_15.16_spmd.clone, body=%wide.region_13.15_spmd.clone.sunk | while | flops 929765376 | bytes 20964980 | solution.py:45
  1756.2 10.8 fusion.143
  1777.6 10.8 fusion.143
  1798.9 10.8 fusion.143
  1820.3 10.8 fusion.143
  1841.6 10.8 fusion.143
  1863.0 10.8 fusion.143
  1916.7 65.4 %psum.31 = f32[16]{0:T(128)S(1)} all-reduce(f32[16]{0:T(128)S(1)} %multiply_reduce_fusion), channel_id=1, replica_groups=mesh['row'=16,'col'=8] {'row','col'}, use_global_device_ids=true, to_apply=%region_17.18 | all-reduce | flops 16 | bytes 128 | tf_op jit(solution)/shard_map/psum | solution.py:81
  (109 shorter events, 296.0 us)
Async XLA Ops:
  7.2 310.6 %all-gather.7.cloned.1.call-start = ((), (), s32[]{:S(2)}) async-start(), calls=%async_computation.1 | async-start | bytes 3170304 | tf_op jit(solution)/shard_map/all_gather | solution.py:70
  7.9 617.3 %all-gather.5.cloned.1.call-start = ((), (), s32[]{:S(2)}) async-start(), calls=%async_computation | async-start | bytes 3170304 | tf_op jit(solution)/shard_map/all_gather | solution.py:61
  9.4 618.0 %copy-start = (f32[384,16]{0,1:T(8,128)S(1)}, f32[384,16]{0,1:T(8,128)}, u32[]{:S(2)}) copy-start(f32[384,16]{0,1:T(8,128)} %get-tuple-element.401) | copy-start | bytes 73732
  9.4 1109.6 %all-gather.9.cloned.1.call-start = ((), (), s32[]{:S(2)}) async-start(), calls=%async_computation.2 | async-start | bytes 3170304 | tf_op jit(solution)/shard_map/all_gather | solution.py:70
  627.4 185.7 %copy-start.3 = (f32[384,16]{0,1:T(8,128)S(1)}, f32[384,16]{0,1:T(8,128)}, u32[]{:S(2)}) copy-start(f32[384,16]{0,1:T(8,128)} %param.12) | copy-start | bytes 73732
  627.4 185.7 %copy-start.4 = (f32[384,16]{0,1:T(8,128)S(1)}, f32[384,16]{0,1:T(8,128)}, u32[]{:S(2)}) copy-start(f32[384,16]{0,1:T(8,128)} %param.11) | copy-start | bytes 73732
  813.8 926.4 %all-gather.11.cloned.1.call-start = ((), (), s32[]{:S(2)}) async-start(), calls=%async_computation.3 | async-start | bytes 3170304 | tf_op jit(solution)/shard_map/all_gather | solution.py:70
  1124.4 184.4 %copy-start.1 = (f32[384,16]{0,1:T(8,128)S(1)}, f32[384,16]{0,1:T(8,128)}, u32[]{:S(2)}) copy-start(f32[384,16]{0,1:T(8,128)} %add_subtract_fusion) | copy-start | bytes 73732
  1745.6 171.0 %copy-start.2 = (f32[384,16]{0,1:T(8,128)S(1)}, f32[384,16]{0,1:T(8,128)}, u32[]{:S(2)}) copy-start(f32[384,16]{0,1:T(8,128)} %multiply_add_fusion.2) | copy-start | bytes 73732
Sparse Core Ops, SparseCore 0:
  9.7 308.0 all-gather.6
  320.1 305.0 all-gather.4
  813.9 305.0 all-gather.8
  1438.1 302.0 all-gather.10
where the time goes:
time: 1990 us
  waiting for transfers between devices  1220 us (61%)
  matrix products  457 us (23%)
  blocking collectives  194 us (10%)
  local copies, waits for them, and re-layouts  70.5 us (4%)
  loops' own time  29.7 us (1%)
    all_gather x3, waiting for transfers between devices, operate(): lax.all_gather(vectors, ('row', 'col'), axis=0, tiled=True)  916 us
    all_gather x1, waiting for transfers between devices, shards(): all_pts = lax.all_gather(scaled, ('row', 'col'), axis=0, tiled=True)  302 us
    dot_general x24, matrix products, matern_apply(): return jnp.dot(kernel, vectors, precision=lax.Precision.HIGHEST)  260 us
    dot_general x24, matrix products, matern_kernel(): crossed = jnp.dot(left_pts, right_pts.T, precision=lax.Precision.HIGHEST)  197 us
    psum x2, blocking collectives, residual_norm(): return lax.psum(col_sums(current, current), ('row', 'col'))  128 us
    psum x1, blocking collectives, shards(): curve = lax.psum(col_sums(direction, image), ('row', 'col'))  65.4 us
    dynamic_slice x24, local copies, waits for them, and re-layouts, fold_blocks(): result, unused = lax.scan(advance, running, (pts_blocks, vec_blocks))  52.1 us
  transfers between devices with their start and end apart: 4, of which 4 were waited for; matrix products, arithmetic and copies ran while one was open for 0% of the time, Pallas kernels for 0%

commit v1 on v0

v1 whole, which is shorter than its diff:
```python
import math

import jax
import jax.numpy as jnp
from jax import lax
from jax.experimental import pallas as pl
from jax.experimental.pallas import tpu as pltpu
from jax.sharding import PartitionSpec as P

MESH = pl.DeviceIdType.MESH
F32, BF16 = jnp.float32, jnp.bfloat16
NOISE_VAR = 0.5
LN2 = math.log(2.0)
DIST_SCALE = math.sqrt(5.0) / LN2
VECS = 16
DEPTH = 128
CHUNK = 768
PIECE = 1024
SUB = 256
KEPT = 1


def split3(x):
    first = x.astype(BF16)
    rest = x - first.astype(F32)
    second = rest.astype(BF16)
    third = (rest - second.astype(F32)).astype(BF16)
    return first, second, third


def stacked(z, left):
    a, b, c = split3(z)
    qa, qb, qc = split3(jnp.sum(z * z, axis=0, keepdims=True))
    row = lax.broadcasted_iota(jnp.int32, z.shape, 0)
    base = 0 if left else 3
    tail = jnp.where(row == base, qa.astype(F32), 0.0)
    tail = jnp.where(row == base + 1, qb.astype(F32), tail)
    tail = jnp.where(row == base + 2, qc.astype(F32), tail)
    other = 3 - base
    tail = jnp.where((row >= other) & (row < other + 3), 1.0, tail)
    a, b, c = a.astype(F32), b.astype(F32), c.astype(F32)
    zero = jnp.zeros_like(tail)
    if left:
        return jnp.concatenate([a, a, b, b, a, c, tail, zero], axis=0)
    a, b, c = -2.0 * a, -2.0 * b, -2.0 * c
    return jnp.concatenate([a, b, a, b, c, a, tail, zero], axis=0)


def matern(s):
    s = jnp.maximum(s, 1e-30)
    dist = s * lax.rsqrt(s)
    shifted = dist + 1.5 / LN2
    return (shifted * shifted + 0.75 / LN2**2) * jnp.exp2(math.log2(LN2**2 / 3.0) - dist)


def make_kernel(rows_n, cols_n, own):
    span = rows_n * own
    wide = cols_n * own
    n_chunks = wide // CHUNK
    n_pieces = span // PIECE
    per_chunk = CHUNK // own
    slots = 3

    def kernel(
        pts_ref, init_ref, targ_ref, scale_ref,
        sol_ref, res_ref, low_hbm,
        high, low, stage, left, right, vecs, first_own, first_all, right_all,
        vec_own, vec_all, part, part_all, dot_a, dot_a_all, dot_b, dot_b_all,
        col_send, col_recv, row_send, row_recv, stage_sem,
    ):
        my_row, my_col = lax.axis_index("row"), lax.axis_index("col")

        barrier = pltpu.get_barrier_semaphore()

        @pl.loop(1, rows_n)
        def _(k):
            pl.semaphore_signal(
                barrier, inc=1, device_id=(lax.rem(my_row + k, rows_n), my_col), device_id_type=MESH
            )

        @pl.loop(1, cols_n)
        def _(k):
            pl.semaphore_signal(
                barrier, inc=1, device_id=(my_row, lax.rem(my_col + k, cols_n)), device_id_type=MESH
            )

        pl.semaphore_wait(barrier, rows_n - 1 + cols_n - 1)

        def to_rows(phase, src, dst, k):
            return pltpu.make_async_remote_copy(
                src_ref=src, dst_ref=dst.at[my_row],
                send_sem=row_send.at[phase, k], recv_sem=row_recv.at[phase, k],
                device_id=(lax.rem(my_row + k, rows_n), my_col), device_id_type=MESH,
            )

        def to_cols(phase, src, dst, k):
            return pltpu.make_async_remote_copy(
                src_ref=src, dst_ref=dst.at[my_col],
                send_sem=col_send.at[phase, k], recv_sem=col_recv.at[phase, k],
                device_id=(my_row, lax.rem(my_col + k, cols_n)), device_id_type=MESH,
            )

        def start_all(make, phase, src, dst, count):
            @pl.loop(1, count)
            def _(k):
                make(phase, src, dst, k).start()

        def wait_all(make, phase, src, dst, count):
            @pl.loop(1, count)
            def _(k):
                make(phase, src, dst, k).wait()

        z_own = pts_ref[...] / scale_ref[...] * DIST_SCALE
        first_own[0:VECS, :] = z_own
        first_own[VECS:, :] = init_ref[...]
        points_own = first_own.at[pl.ds(0, VECS)]
        start_all(to_cols, 0, points_own, right_all, cols_n)
        start_all(to_rows, 0, first_own, first_all, rows_n)
        first_all[my_row] = first_own[...]
        right_all[my_col] = z_own
        wait_all(to_cols, 0, points_own, right_all, cols_n)
        for slot in range(cols_n):
            right[:, slot * own:(slot + 1) * own] = stacked(right_all[slot], False).astype(BF16)
        wait_all(to_rows, 0, first_own, first_all, rows_n)

        def put_vecs(slot, block):
            here = pl.ds(pl.multiple_of(slot * own, 128), own)
            a, b, c = split3(block)
            vecs[0:VECS, here] = a
            vecs[VECS:2 * VECS, here] = b
            vecs[2 * VECS:, here] = c

        @pl.loop(0, rows_n)
        def _(slot):
            here = pl.ds(pl.multiple_of(slot * own, 128), own)
            left[here, :] = stacked(first_all[slot, 0:VECS], True).T.astype(BF16)
            put_vecs(slot, first_all[slot, VECS:])

        def fold(acc, acc_low):
            return acc[0:VECS] + acc[VECS:2 * VECS] + acc[2 * VECS:] + acc_low

        def send_part(call, chunk, total):
            for n in range(per_chunk):
                owner = chunk * per_chunk + n
                part[call, owner] = total[:, n * own:(n + 1) * own]

                @pl.when(owner != my_col)
                def _():
                    part_copy(call, owner).start()

        def part_copy(call, owner):
            k = lax.rem(owner - my_col + cols_n, cols_n)
            return to_cols(1 + call, part.at[call, owner], part_all.at[call], k)

        def reduced(call, block):
            @pl.loop(1, cols_n)
            def _(k):
                part_copy(call, lax.rem(my_col + k, cols_n)).wait()
            part_all[call, my_col] = part[call, my_col]
            total = part_all[call, 0]
            for slot in range(1, cols_n):
                total = total + part_all[call, slot]
            return total + NOISE_VAR * block

        def low_copy(chunk, piece, slot, out):
            away = low_hbm.at[chunk - KEPT, piece]
            here = stage.at[slot]
            if out:
                return pltpu.make_async_copy(here, away, stage_sem.at[slot])
            return pltpu.make_async_copy(away, here, stage_sem.at[slot])

        for chunk in range(n_chunks):
            cols = slice(chunk * CHUNK, (chunk + 1) * CHUNK)

            def make_piece(piece, carry, chunk=chunk, cols=cols):
                acc, acc_low = carry
                if chunk >= KEPT:
                    count = (chunk - KEPT) * n_pieces + piece
                    slot = lax.rem(count, slots)

                    @pl.when(count >= slots)
                    def _():
                        low_copy(chunk, piece, slot, True).wait()
                for sub in range(PIECE // SUB):
                    rows = pl.ds(pl.multiple_of(piece * PIECE + sub * SUB, SUB), SUB)
                    m = matern(jnp.dot(left[rows, :], right[:, cols], preferred_element_type=F32))
                    h = m.astype(BF16)
                    l = (m - h.astype(F32)).astype(BF16)
                    high[rows, cols] = h
                    if chunk < KEPT:
                        low[rows, cols] = l
                    else:
                        stage[slot, sub * SUB:(sub + 1) * SUB, :] = l
                    acc = acc + jnp.dot(vecs[:, rows], h, preferred_element_type=F32)
                    acc_low = acc_low + jnp.dot(vecs[0:VECS, rows], l, preferred_element_type=F32)
                if chunk >= KEPT:
                    low_copy(chunk, piece, slot, True).start()
                return acc, acc_low

            acc, acc_low = lax.fori_loop(
                0, n_pieces, make_piece,
                (jnp.zeros((3 * VECS, CHUNK), F32), jnp.zeros((VECS, CHUNK), F32)),
            )
            send_part(0, chunk, fold(acc, acc_low))

        total_pieces = (n_chunks - KEPT) * n_pieces
        for slot in range(slots):
            low_copy(KEPT, 0, slot, True).wait()

        def prefetch(count):
            low_copy(KEPT + count // n_pieces, lax.rem(count, n_pieces), lax.rem(count, slots), False).start()

        def apply(call):
            for chunk in range(n_chunks):
                cols = slice(chunk * CHUNK, (chunk + 1) * CHUNK)
                if chunk < KEPT:
                    acc = jnp.dot(vecs[...], high[:, cols], preferred_element_type=F32)
                    acc_low = jnp.dot(vecs[0:VECS, :], low[:, cols], preferred_element_type=F32)
                else:
                    def use_piece(piece, carry, chunk=chunk, cols=cols):
                        acc, acc_low = carry
                        rows = pl.ds(pl.multiple_of(piece * PIECE, PIECE), PIECE)
                        acc = acc + jnp.dot(vecs[:, rows], high[rows, cols], preferred_element_type=F32)
                        count = (chunk - KEPT) * n_pieces + piece
                        slot = lax.rem(count, slots)
                        low_copy(chunk, piece, slot, False).wait()
                        acc_low = acc_low + jnp.dot(
                            vecs[0:VECS, rows], stage[slot], preferred_element_type=F32
                        )

                        @pl.when(count + slots < total_pieces)
                        def _():
                            prefetch(count + slots)
                        return acc, acc_low

                    acc, acc_low = lax.fori_loop(
                        0, n_pieces, use_piece,
                        (jnp.zeros((3 * VECS, CHUNK), F32), jnp.zeros((VECS, CHUNK), F32)),
                    )
                send_part(call, chunk, fold(acc, acc_low))

        def spread(phase, block):
            vec_own[phase] = block
            start_all(to_rows, 1 + phase, vec_own.at[phase], vec_all.at[phase], rows_n)
            vec_all[phase, my_row] = block
            wait_all(to_rows, 1 + phase, vec_own.at[phase], vec_all.at[phase], rows_n)

            @pl.loop(0, rows_n)
            def _(slot):
                put_vecs(slot, vec_all[phase, slot])

        def lanes(x):
            total = x[:, 0:128]
            for n in range(1, own // 128):
                total = total + x[:, n * 128:(n + 1) * 128]
            return total

        def dots(phase, pairs):
            size = VECS * len(pairs)
            for n, (x, y) in enumerate(pairs):
                dot_a[phase, n * VECS:(n + 1) * VECS, :] = lanes(x * y)
            used = pl.ds(0, size)
            mine = dot_a.at[phase, used]
            theirs = dot_a_all.at[phase, :, used]
            start_all(to_cols, 4 + phase, mine, theirs, cols_n)
            dot_a_all[phase, my_col, 0:size] = dot_a[phase, 0:size]
            wait_all(to_cols, 4 + phase, mine, theirs, cols_n)
            total = dot_a_all[phase, 0, 0:size]
            for slot in range(1, cols_n):
                total = total + dot_a_all[phase, slot, 0:size]
            dot_b[phase, 0:size] = total
            mine = dot_b.at[phase, used]
            theirs = dot_b_all.at[phase, :, used]
            start_all(to_rows, 3 + phase, mine, theirs, rows_n)
            dot_b_all[phase, my_row, 0:size] = total
            wait_all(to_rows, 3 + phase, mine, theirs, rows_n)
            total = dot_b_all[phase, 0, 0:size]
            for slot in range(1, rows_n):
                total = total + dot_b_all[phase, slot, 0:size]
            total = jnp.sum(total, axis=1, keepdims=True)
            return [total[n * VECS:(n + 1) * VECS] for n in range(len(pairs))]

        for count in range(slots):
            prefetch(count)
        init = init_ref[...]
        res0 = targ_ref[...] - reduced(0, init)
        spread(0, res0)
        apply(1)
        for count in range(slots):
            prefetch(count)
        image0 = reduced(1, res0)
        norm0, curve0 = dots(0, [(res0, res0), (res0, image0)])
        alpha0 = norm0 / curve0
        res1 = res0 - alpha0 * image0
        spread(1, res1)
        apply(2)
        half = reduced(2, res1)
        norm1, own_curve, cross = dots(1, [(res1, res1), (res1, half), (res1 + res1, image0)])
        beta0 = norm1 / norm0
        curve1 = own_curve + beta0 * cross + beta0 * beta0 * curve0
        alpha1 = norm1 / curve1
        sol_ref[...] = init + alpha0 * res0 + alpha1 * (res1 + beta0 * res0)
        res_ref[...] = res1 - alpha1 * (half + beta0 * image0)

    def scratch():
        return [
            pltpu.VMEM((span, wide), BF16),
            pltpu.VMEM((span, KEPT * CHUNK), BF16),
            pltpu.VMEM((slots, PIECE, CHUNK), BF16),
            pltpu.VMEM((span, DEPTH), BF16),
            pltpu.VMEM((DEPTH, wide), BF16),
            pltpu.VMEM((3 * VECS, span), BF16),
            pltpu.VMEM((2 * VECS, own), F32),
            pltpu.VMEM((rows_n, 2 * VECS, own), F32),
            pltpu.VMEM((cols_n, VECS, own), F32),
            pltpu.VMEM((2, VECS, own), F32),
            pltpu.VMEM((2, rows_n, VECS, own), F32),
            pltpu.VMEM((3, cols_n, VECS, own), F32),
            pltpu.VMEM((3, cols_n, VECS, own), F32),
            pltpu.VMEM((2, 3 * VECS, 128), F32),
            pltpu.VMEM((2, cols_n, 3 * VECS, 128), F32),
            pltpu.VMEM((2, 3 * VECS, 128), F32),
            pltpu.VMEM((2, rows_n, 3 * VECS, 128), F32),
            pltpu.SemaphoreType.DMA((6, cols_n)),
            pltpu.SemaphoreType.DMA((6, cols_n)),
            pltpu.SemaphoreType.DMA((5, rows_n)),
            pltpu.SemaphoreType.DMA((5, rows_n)),
            pltpu.SemaphoreType.DMA((slots,)),
        ]

    vmem = pl.BlockSpec(memory_space=pltpu.VMEM)
    return pl.pallas_call(
        kernel,
        out_shape=[
            jax.ShapeDtypeStruct((VECS, own), F32),
            jax.ShapeDtypeStruct((VECS, own), F32),
            jax.ShapeDtypeStruct((n_chunks - KEPT, n_pieces, PIECE, CHUNK), BF16),
        ],
        in_specs=[vmem] * 4,
        out_specs=[vmem, vmem, pl.BlockSpec(memory_space=pl.ANY)],
        scratch_shapes=scratch(),
        compiler_params=pltpu.CompilerParams(
            collective_id=0, has_side_effects=True, vmem_limit_bytes=60 * 2**20
        ),
        name="conjugate_gradients",
    )


def solution(mesh):
    rows_n, cols_n = mesh.shape["row"], mesh.shape["col"]

    def shards(points, targets, initial, lengthscale):
        call = make_kernel(rows_n, cols_n, points.shape[0])
        sol, res, _ = call(points.T, initial.T, targets.T, lengthscale[:, None])
        return sol.T, res.T

    spec = P(("row", "col"), None)
    return jax.shard_map(
        shards, mesh=mesh, in_specs=(spec, spec, spec, P()), out_specs=(spec, spec), check_vma=False
    )
```

time: 1990 us -> 170 us (0.09)
  waiting for transfers between devices: 1220 us -> 0 us
  matrix products: 457 us -> 0 us
  blocking collectives: 194 us -> 0 us
  Pallas kernels: 0 us -> 165 us
  local copies, waits for them, and re-layouts: 70.5 us -> 4.02 us
  loops' own time: 29.7 us -> 0 us
    all_gather x4 -> x0, waiting for transfers between devices: 1220 us -> none  [the longest x3 916 us: operate(): lax.all_gather(vectors, ('row', 'col'), axis=0, tiled=True)]
    dot_general x48 -> x0, matrix products: 457 us -> none  [the longest x24 260 us: matern_apply(): return jnp.dot(kernel, vectors, precision=lax.Precision.HIGHEST)]
    psum x3 -> x0, blocking collectives: 194 us -> none  [the longest x2 128 us: residual_norm(): return lax.psum(col_sums(current, current), ('row', 'col'))]
    pallas_call x0 -> x1, Pallas kernels: none -> 165 us  [shards(): sol, res, _ = call(points.T, initial.T, targets.T, lengthscale[:, None])]
    dynamic_slice x24 -> x0, local copies, waits for them, and re-layouts: 52.1 us -> none  [fold_blocks(): result, unused = lax.scan(advance, running, (pts_blocks, vec_blocks))]
    another operation x3 -> x0, loops' own time: 29.7 us -> none  [fold_blocks(): result, unused = lax.scan(advance, running, (pts_blocks, vec_blocks))]
  transfers between devices with their start and end apart: 4 -> 0, of which waited for: 4 -> 0; matrix products, arithmetic and copies ran while one was open for 0% -> 0% of each run, Pallas kernels for 0% -> 0%
where the time goes in v1:
time: 170 us
  Pallas kernels  165 us (97%)
  local copies, waits for them, and re-layouts  4.02 us (2%)
    pallas_call x1, Pallas kernels, shards(): sol, res, _ = call(points.T, initial.T, targets.T, lengthscale[:, None])  165 us

profile of v1, /device:TPU:1, one launch (start us, length us, event | category | flops | bytes accessed | tf_op | source)
XLA Modules:
  0.0 169.8 jit_solution(9029441205552670225)
XLA Ops:
  0.6 1.3 copy.6.scale_ref
  2.0 165.2 %conjugate_gradients.1 = (f32[16,384]{1,0:T(8,128)}, f32[16,384]{1,0:T(8,128)}, bf16[3,6,1024,768]{3,2,1,0:T(8,128)(2,1)}) custom-call(f32[16,384]{1,0:T(8,128)} %bitcast.8, f32[16,384]{1,0:T(8,128)} %bitcast.9, f32[16,384]{1,0:T(8,128)} %bitcast.10, f32[16,1]{1,0:T(8,128)} %copy.6.scale_ref), custom_call_target="tpu_custom_call" | custom-call | tf_op jit(solution)/shard_map/conjugate_gradients/pallas_call | solution.py:354
  167.2 1.3 copy.9
  168.5 1.3 copy.10

commit v2 on v1

v2 whole, which is shorter than its diff:
```python
import math

import jax
import jax.numpy as jnp
from jax import lax
from jax.experimental import pallas as pl
from jax.experimental.pallas import tpu as pltpu
from jax.sharding import PartitionSpec as P

MESH = pl.DeviceIdType.MESH
F32, BF16 = jnp.float32, jnp.bfloat16
NOISE_VAR = 0.5
LN2 = math.log(2.0)
DIST_SCALE = math.sqrt(5.0) / LN2
VECS = 16
DEPTH = 128
CHUNK = 768
PIECE = 768
SUB = 256
STAGES = 3
EARLY = 3
LAG = 8


def split3(x):
    first = x.astype(BF16)
    rest = x - first.astype(F32)
    second = rest.astype(BF16)
    third = (rest - second.astype(F32)).astype(BF16)
    return first, second, third


def stacked(z, left):
    a, b, c = split3(z)
    qa, qb, qc = split3(jnp.sum(z * z, axis=0, keepdims=True))
    row = lax.broadcasted_iota(jnp.int32, z.shape, 0)
    base = 0 if left else 3
    tail = jnp.where(row == base, qa.astype(F32), 0.0)
    tail = jnp.where(row == base + 1, qb.astype(F32), tail)
    tail = jnp.where(row == base + 2, qc.astype(F32), tail)
    other = 3 - base
    tail = jnp.where((row >= other) & (row < other + 3), 1.0, tail)
    a, b, c = a.astype(F32), b.astype(F32), c.astype(F32)
    zero = jnp.zeros_like(tail)
    if left:
        return jnp.concatenate([a, a, b, b, a, c, tail, zero], axis=0)
    a, b, c = -2.0 * a, -2.0 * b, -2.0 * c
    return jnp.concatenate([a, b, a, b, c, a, tail, zero], axis=0)


def matern(s):
    s = jnp.maximum(s, 1e-30)
    dist = s * lax.rsqrt(s)
    shifted = dist + 1.5 / LN2
    return (shifted * shifted + 0.75 / LN2**2) * jnp.exp2(math.log2(LN2**2 / 3.0) - dist)


def make_kernel(rows_n, cols_n, own):
    span = rows_n * own
    wide = cols_n * own
    n_chunks = wide // CHUNK
    n_pieces = span // PIECE
    pair = CHUNK // own
    turns = n_chunks
    kept_n = n_pieces // turns

    def is_kept(piece, chunk):
        return (piece + chunk) % turns == 0

    def kept_at(piece, chunk):
        return chunk * kept_n + piece // turns

    def kernel(
        pts_ref, init_ref, targ_ref, scale_ref,
        sol_ref, res_ref, low_hbm,
        high, low, stage, left, right, vecs, acc_ref, first_own, first_all, right_all,
        vec_own, vec_all, part, part_all, dot_a, dot_a_all, dot_b, dot_b_all,
        col_send, col_recv, row_send, row_recv, stage_sem,
    ):
        my_row, my_col = lax.axis_index("row"), lax.axis_index("col")
        first_turn = lax.rem(my_row, turns)
        my_turn = lax.rem(my_col // pair - first_turn + turns, turns)
        my_slot = my_turn * (rows_n // turns) + my_row // turns
        my_place = my_turn * pair + lax.rem(my_col, pair)

        barrier = pltpu.get_barrier_semaphore()

        @pl.loop(1, rows_n)
        def _(k):
            pl.semaphore_signal(
                barrier, inc=1, device_id=(lax.rem(my_row + k, rows_n), my_col), device_id_type=MESH
            )

        @pl.loop(1, cols_n)
        def _(k):
            pl.semaphore_signal(
                barrier, inc=1, device_id=(my_row, lax.rem(my_col + k, cols_n)), device_id_type=MESH
            )

        z_own = pts_ref[...] / scale_ref[...] * DIST_SCALE
        first_own[0:VECS, :] = z_own
        first_own[VECS:, :] = init_ref[...]
        pl.semaphore_wait(barrier, rows_n - 1 + cols_n - 1)

        def to_rows(phase, src, dst, k, slot):
            return pltpu.make_async_remote_copy(
                src_ref=src, dst_ref=dst.at[slot],
                send_sem=row_send.at[phase, k], recv_sem=row_recv.at[phase, slot],
                device_id=(lax.rem(my_row + k, rows_n), my_col), device_id_type=MESH,
            )

        def to_cols(phase, src, dst, k, slot):
            return pltpu.make_async_remote_copy(
                src_ref=src, dst_ref=dst.at[slot],
                send_sem=col_send.at[phase, k], recv_sem=col_recv.at[phase, slot],
                device_id=(my_row, lax.rem(my_col + k, cols_n)), device_id_type=MESH,
            )

        def start_all(make, phase, src, dst, count, slot):
            @pl.loop(1, count)
            def _(k):
                make(phase, src, dst, k, slot).start()

        def sent_all(make, phase, src, dst, count):
            @pl.loop(1, count)
            def _(k):
                make(phase, src, dst, k, 0).wait_send()

        def arrived(make, phase, src, dst, slot, mine):
            @pl.when(slot != mine)
            def _():
                make(phase, src, dst, 1, slot).wait_recv()

        points_own = first_own.at[pl.ds(0, VECS)]
        start_all(to_cols, 0, points_own, right_all, cols_n, my_place)
        start_all(to_rows, 0, first_own, first_all, rows_n, my_slot)
        first_all[my_slot] = first_own[...]
        right_all[my_place] = z_own

        def put_vecs(slot, block):
            here = pl.ds(pl.multiple_of(slot * own, 128), own)
            a, b, c = split3(block)
            vecs[0:VECS, here] = a
            vecs[VECS:2 * VECS, here] = b
            vecs[2 * VECS:, here] = c

        def part_copy(call, owner, sender):
            k = lax.rem(owner - my_col + cols_n, cols_n)
            return to_cols(1 + call, part.at[call, owner], part_all.at[call], k, sender)

        def send_part(call, turn, acc):
            total = acc[0:VECS] + acc[VECS:2 * VECS] + acc[2 * VECS:3 * VECS] + acc[3 * VECS:]
            for n in range(pair):
                owner = lax.rem(first_turn + turn, turns) * pair + n
                part[call, owner] = total[:, n * own:(n + 1) * own]

                @pl.when(owner != my_col)
                def _():
                    part_copy(call, owner, my_col).start()

        def reduced(call, block):
            @pl.loop(1, cols_n)
            def _(k):
                part_copy(call, lax.rem(my_col + 1, cols_n), lax.rem(my_col + k, cols_n)).wait_recv()
            part_all[call, my_col] = part[call, my_col]
            total = part_all[call, 0]
            for slot in range(1, cols_n):
                total = total + part_all[call, slot]
            return total + NOISE_VAR * block

        def owner_step(call, turn):
            @pl.when(my_turn == turn)
            def _():
                if call == 0:
                    block = targ_ref[...] - reduced(0, init_ref[...])
                else:
                    block = reduced(1, vec_own[0])
                vec_own[call] = block
                vec_all[call, my_slot] = block
                start_all(to_rows, 1 + call, vec_own.at[call], vec_all.at[call], rows_n, my_slot)

        def take_piece(call, piece):
            for n in range(2):
                slot = piece * 2 + n
                arrived(to_rows, 1 + call, vec_own.at[call], vec_all.at[call], slot, my_slot)
                put_vecs(slot, vec_all[call, slot])

        @pl.loop(0, n_chunks)
        def _(chunk):
            cols = pl.ds(pl.multiple_of(chunk * CHUNK, CHUNK), CHUNK)
            for n in range(pair):
                place = chunk * pair + n
                arrived(to_cols, 0, points_own, right_all, place, my_place)
                right[:, pl.ds(pl.multiple_of(place * own, 128), own)] = stacked(right_all[place], False).astype(BF16)
            acc_ref[0] = jnp.zeros((4 * VECS, CHUNK), F32)

            @pl.loop(0, n_pieces)
            def _(turn):
                piece = lax.rem(my_slot // 2 + turn, n_pieces)

                @pl.when(chunk == 0)
                def _():
                    for n in range(2):
                        slot = piece * 2 + n
                        arrived(to_rows, 0, first_own, first_all, slot, my_slot)
                        here = pl.ds(pl.multiple_of(slot * own, 128), own)
                        left[here, :] = stacked(first_all[slot, 0:VECS], True).T.astype(BF16)
                        put_vecs(slot, first_all[slot, VECS:])

                count = chunk * n_pieces + turn
                slot = lax.rem(count, STAGES)

                @pl.when(count >= STAGES)
                def _():
                    pltpu.make_async_copy(stage.at[slot], low.at[0], stage_sem.at[slot]).wait()

                acc = acc_low = None
                for sub in range(PIECE // SUB):
                    rows = pl.ds(pl.multiple_of(piece * PIECE + sub * SUB, SUB), SUB)
                    m = matern(jnp.dot(left[rows, :], right[:, cols], preferred_element_type=F32))
                    h = m.astype(BF16)
                    l = (m - h.astype(F32)).astype(BF16)
                    high[rows, cols] = h
                    stage[slot, sub * SUB:(sub + 1) * SUB, :] = l
                    more = jnp.dot(vecs[:, rows], h, preferred_element_type=F32)
                    more_low = jnp.dot(vecs[0:VECS, rows], l, preferred_element_type=F32)
                    acc = more if acc is None else acc + more
                    acc_low = more_low if acc_low is None else acc_low + more_low
                acc_ref[0, 0:3 * VECS] += acc
                acc_ref[0, 3 * VECS:] += acc_low

                kept = is_kept(piece, chunk)

                @pl.when(kept)
                def _():
                    pltpu.make_async_copy(
                        stage.at[slot], low.at[kept_at(piece, chunk)], stage_sem.at[slot]
                    ).start()

                @pl.when(jnp.logical_not(kept))
                def _():
                    pltpu.make_async_copy(stage.at[slot], low_hbm.at[chunk, piece], stage_sem.at[slot]).start()

            send_part(0, chunk, acc_ref[0])
            for turn in range(n_chunks - 1):
                @pl.when(chunk == turn + 1)
                def _():
                    owner_step(0, turn)

        for slot in range(STAGES):
            pltpu.make_async_copy(stage.at[slot], low.at[0], stage_sem.at[slot]).wait()

        early = [(piece, chunk) for piece in range(EARLY) for chunk in range(n_chunks)]
        late = [(piece, chunk) for chunk in range(n_chunks) for piece in range(EARLY, n_pieces)]
        units = early + late
        far = [unit for unit in units if not is_kept(*unit)]

        def fetch(count):
            piece, chunk = far[count % len(far)]
            slot = count % STAGES
            return pltpu.make_async_copy(low_hbm.at[chunk, piece], stage.at[slot], stage_sem.at[slot])

        def product(call, fetched, last, hooks):
            for number, (piece, chunk) in enumerate(units):
                for hook in hooks.get(number, ()):
                    hook()
                if chunk == 0:
                    take_piece(call - 1, piece)
                rows = slice(piece * PIECE, (piece + 1) * PIECE)
                cols = slice(chunk * CHUNK, (chunk + 1) * CHUNK)
                acc = jnp.dot(vecs[:, rows], high[rows, cols], preferred_element_type=F32)
                if is_kept(piece, chunk):
                    below = low[kept_at(piece, chunk)]
                else:
                    fetch(fetched).wait()
                    below = stage[fetched % STAGES]
                acc_low = jnp.dot(vecs[0:VECS, rows], below, preferred_element_type=F32)
                if not is_kept(piece, chunk):
                    if not (last and fetched + STAGES >= 2 * len(far)):
                        fetch(fetched + STAGES).start()
                    fetched += 1
                if piece == 0:
                    acc_ref[chunk, 0:3 * VECS] = acc
                    acc_ref[chunk, 3 * VECS:] = acc_low
                else:
                    acc_ref[chunk, 0:3 * VECS] += acc
                    acc_ref[chunk, 3 * VECS:] += acc_low
                if piece == n_pieces - 1:
                    send_part(call, chunk, acc_ref[chunk])
            return fetched

        row_of = lax.broadcasted_iota(jnp.int32, (VECS, 128), 0)
        lane_of = lax.broadcasted_iota(jnp.int32, (VECS, 128), 1)

        def dots_local(phase, pairs):
            line = jnp.zeros((1, 128), F32)
            for n, (x, y) in enumerate(pairs):
                value = jnp.sum(x * y, axis=1, keepdims=True)
                here = lane_of == row_of + n * VECS
                line = line + jnp.sum(jnp.where(here, value, 0.0), axis=0, keepdims=True)
            block = jnp.broadcast_to(line, (8, 128))
            dot_a[phase] = block
            dot_a_all[phase, my_col] = block
            start_all(to_cols, 4 + phase, dot_a.at[phase], dot_a_all.at[phase], cols_n, my_col)

        def dots_row(phase):
            @pl.loop(1, cols_n)
            def _(k):
                slot = lax.rem(my_col + k, cols_n)
                to_cols(4 + phase, dot_a.at[phase], dot_a_all.at[phase], 1, slot).wait_recv()
            total = dot_a_all[phase, 0]
            for slot in range(1, cols_n):
                total = total + dot_a_all[phase, slot]
            dot_b[phase] = total
            dot_b_all[phase, my_row] = total
            start_all(to_rows, 3 + phase, dot_b.at[phase], dot_b_all.at[phase], rows_n, my_row)

        def dots_whole(phase, count):
            @pl.loop(1, rows_n)
            def _(k):
                slot = lax.rem(my_row + k, rows_n)
                to_rows(3 + phase, dot_b.at[phase], dot_b_all.at[phase], 1, slot).wait_recv()
            total = dot_b_all[phase, 0]
            for slot in range(1, rows_n):
                total = total + dot_b_all[phase, slot]
            line = jnp.broadcast_to(total[0:1], (VECS, 128))
            return [
                jnp.sum(jnp.where(lane_of == row_of + n * VECS, line, 0.0), axis=1, keepdims=True)
                for n in range(count)
            ]

        def sent_before():
            sent_all(to_cols, 0, points_own, right_all, cols_n)
            sent_all(to_rows, 0, first_own, first_all, rows_n)
            for call in range(2):
                sent_parts(call)
                sent_all(to_rows, 1 + call, vec_own.at[call], vec_all.at[call], rows_n)

        def sent_parts(call):
            @pl.loop(1, cols_n)
            def _(k):
                part_copy(call, lax.rem(my_col + k, cols_n), 0).wait_send()

        def hooks_after(call):
            found = {}
            for turn in range(n_chunks):
                done = len(early) + (turn + 1) * (n_pieces - EARLY)
                at = done + LAG - len(units)
                if call == 0:
                    at = LAG if turn == n_chunks - 1 else None
                if at is not None and at >= 0:
                    found.setdefault(at, []).append(lambda turn=turn: owner_step(call, turn))
            return found

        def hooks_within(call):
            found = {}
            for turn in range(n_chunks):
                done = len(early) + (turn + 1) * (n_pieces - EARLY)
                if done + LAG < len(units):
                    found.setdefault(done + LAG, []).append(lambda turn=turn: owner_step(call, turn))
            return found

        def merged(*tables):
            found = {}
            for table in tables:
                for at, hooks in table.items():
                    found.setdefault(at, []).extend(hooks)
            return found

        for count in range(STAGES):
            fetch(count).start()
        fetched = product(1, 0, False, merged(hooks_after(0), hooks_within(1)))
        fetched = product(2, fetched, True, merged(
            hooks_after(1),
            {
                14: [lambda: dots_local(0, [(vec_own[0], vec_own[0]), (vec_own[0], vec_own[1])])],
                18: [sent_before],
                26: [lambda: dots_row(0)],
            },
        ))
        res0, image0 = vec_own[0], vec_own[1]
        norm0, curve0 = dots_whole(0, 2)
        alpha0 = norm0 / curve0
        res1 = res0 - alpha0 * image0
        image1 = reduced(2, image0)
        half = image0 - alpha0 * image1
        dots_local(1, [(res1, res1), (res1, half), (res1 + res1, image0)])
        dots_row(1)
        norm1, own_curve, cross = dots_whole(1, 3)
        beta0 = norm1 / norm0
        curve1 = own_curve + beta0 * cross + beta0 * beta0 * curve0
        alpha1 = norm1 / curve1
        sol_ref[...] = init_ref[...] + alpha0 * res0 + alpha1 * (res1 + beta0 * res0)
        res_ref[...] = res1 - alpha1 * (half + beta0 * image0)
        sent_parts(2)
        for phase in range(2):
            sent_all(to_cols, 4 + phase, dot_a.at[phase], dot_a_all.at[phase], cols_n)
            sent_all(to_rows, 3 + phase, dot_b.at[phase], dot_b_all.at[phase], rows_n)

    def scratch():
        return [
            pltpu.VMEM((span, wide), BF16),
            pltpu.VMEM((n_chunks * kept_n, PIECE, CHUNK), BF16),
            pltpu.VMEM((STAGES, PIECE, CHUNK), BF16),
            pltpu.VMEM((span, DEPTH), BF16),
            pltpu.VMEM((DEPTH, wide), BF16),
            pltpu.VMEM((3 * VECS, span), BF16),
            pltpu.VMEM((n_chunks, 4 * VECS, CHUNK), F32),
            pltpu.VMEM((2 * VECS, own), F32),
            pltpu.VMEM((rows_n, 2 * VECS, own), F32),
            pltpu.VMEM((cols_n, VECS, own), F32),
            pltpu.VMEM((2, VECS, own), F32),
            pltpu.VMEM((2, rows_n, VECS, own), F32),
            pltpu.VMEM((3, cols_n, VECS, own), F32),
            pltpu.VMEM((3, cols_n, VECS, own), F32),
            pltpu.VMEM((2, 8, 128), F32),
            pltpu.VMEM((2, cols_n, 8, 128), F32),
            pltpu.VMEM((2, 8, 128), F32),
            pltpu.VMEM((2, rows_n, 8, 128), F32),
            pltpu.SemaphoreType.DMA((6, cols_n)),
            pltpu.SemaphoreType.DMA((6, cols_n)),
            pltpu.SemaphoreType.DMA((5, rows_n)),
            pltpu.SemaphoreType.DMA((5, rows_n)),
            pltpu.SemaphoreType.DMA((STAGES,)),
        ]

    vmem = pl.BlockSpec(memory_space=pltpu.VMEM)
    return pl.pallas_call(
        kernel,
        out_shape=[
            jax.ShapeDtypeStruct((VECS, own), F32),
            jax.ShapeDtypeStruct((VECS, own), F32),
            jax.ShapeDtypeStruct((n_chunks, n_pieces, PIECE, CHUNK), BF16),
        ],
        in_specs=[vmem] * 4,
        out_specs=[vmem, vmem, pl.BlockSpec(memory_space=pl.ANY)],
        scratch_shapes=scratch(),
        compiler_params=pltpu.CompilerParams(
            collective_id=0, has_side_effects=True, vmem_limit_bytes=60 * 2**20
        ),
        name="conjugate_gradients",
    )


def solution(mesh):
    rows_n, cols_n = mesh.shape["row"], mesh.shape["col"]

    def shards(points, targets, initial, lengthscale):
        call = make_kernel(rows_n, cols_n, points.shape[0])
        sol, res, _ = call(points.T, initial.T, targets.T, lengthscale[:, None])
        return sol.T, res.T

    spec = P(("row", "col"), None)
    return jax.shard_map(
        shards, mesh=mesh, in_specs=(spec, spec, spec, P()), out_specs=(spec, spec), check_vma=False
    )
```

time: 170 us -> 135 us (0.79)
  Pallas kernels: 165 us -> 130 us
    pallas_call x1, Pallas kernels: 165 us -> 130 us  [shards(): sol, res, _ = call(points.T, initial.T, targets.T, lengthscale[:, None])]
where the time goes in v2:
time: 135 us; the launch traced here: 134 us
  Pallas kernels  130 us (96%)
  local copies, waits for them, and re-layouts  4.02 us (3%)
    pallas_call x1, Pallas kernels, shards(): sol, res, _ = call(points.T, initial.T, targets.T, lengthscale[:, None])  130 us

profile of v2, /device:TPU:1, one launch (start us, length us, event | category | flops | bytes accessed | tf_op | source)
XLA Modules:
  0.0 134.3 jit_solution(17207411813225502207)
XLA Ops:
  0.6 1.3 copy.6.scale_ref
  2.0 129.6 %conjugate_gradients.1 = (f32[16,384]{1,0:T(8,128)}, f32[16,384]{1,0:T(8,128)}, bf16[4,8,768,768]{3,2,1,0:T(8,128)(2,1)}) custom-call(f32[16,384]{1,0:T(8,128)} %bitcast.8, f32[16,384]{1,0:T(8,128)} %bitcast.9, f32[16,384]{1,0:T(8,128)} %bitcast.10, f32[16,1]{1,0:T(8,128)} %copy.6.scale_ref), custom_call_target="tpu_custom_call" | custom-call | tf_op jit(solution)/shard_map/conjugate_gradients/pallas_call | solution.py:450
  131.6 1.3 %copy.9 = f32[384,16]{0,1:T(8,128)} copy(f32[384,16]{0,1:T(8,128)} %bitcast.7) | data formatting | bytes 49152
  132.9 1.3 %copy.10 = f32[384,16]{0,1:T(8,128)} copy(f32[384,16]{0,1:T(8,128)} %bitcast.6) | data formatting | bytes 49152

commit v3 on v2

--- a/solution.py
+++ b/solution.py
@@ -16,10 +16,11 @@
 DEPTH = 128
 CHUNK = 768
 PIECE = 768
-SUB = 256
-STAGES = 3
+GROUP = 2 * PIECE
+SUB = 512
+STAGES = 4
 EARLY = 3
-LAG = 8
+LAG = 7
 
 
 def split3(x):
@@ -62,25 +63,22 @@
     n_pieces = span // PIECE
     pair = CHUNK // own
     turns = n_chunks
-    kept_n = n_pieces // turns
-
-    def is_kept(piece, chunk):
-        return (piece + chunk) % turns == 0
-
-    def kept_at(piece, chunk):
-        return chunk * kept_n + piece // turns
+    each = rows_n // turns
+
+    def is_kept(group, chunk):
+        return (group + chunk) % turns == 0
 
     def kernel(
         pts_ref, init_ref, targ_ref, scale_ref,
-        sol_ref, res_ref, low_hbm,
+        out_ref, low_hbm,
         high, low, stage, left, right, vecs, acc_ref, first_own, first_all, right_all,
-        vec_own, vec_all, part, part_all, dot_a, dot_a_all, dot_b, dot_b_all,
+        vec_own, vec_all, col_all, part, part_all, dot_a, dot_a_all, dot_b, dot_b_all,
         col_send, col_recv, row_send, row_recv, stage_sem,
     ):
         my_row, my_col = lax.axis_index("row"), lax.axis_index("col")
         first_turn = lax.rem(my_row, turns)
         my_turn = lax.rem(my_col // pair - first_turn + turns, turns)
-        my_slot = my_turn * (rows_n // turns) + my_row // turns
+        my_slot = my_turn * each + my_row // turns
         my_place = my_turn * pair + lax.rem(my_col, pair)
 
         barrier = pltpu.get_barrier_semaphore()
@@ -97,7 +95,11 @@
                 barrier, inc=1, device_id=(my_row, lax.rem(my_col + k, cols_n)), device_id_type=MESH
             )
 
-        z_own = pts_ref[...] / scale_ref[...] * DIST_SCALE
+        square = (VECS, VECS)
+        on_diagonal = lax.broadcasted_iota(jnp.int32, square, 0) == lax.broadcasted_iota(jnp.int32, square, 1)
+        scales = jnp.broadcast_to(scale_ref[...], square)
+        scale = jnp.sum(jnp.where(on_diagonal, scales, 0.0), axis=1, keepdims=True)
+        z_own = pts_ref[...] / scale * DIST_SCALE
         first_own[0:VECS, :] = z_own
         first_own[VECS:, :] = init_ref[...]
         pl.semaphore_wait(barrier, rows_n - 1 + cols_n - 1)
@@ -132,8 +134,19 @@
                 make(phase, src, dst, 1, slot).wait_recv()
 
         points_own = first_own.at[pl.ds(0, VECS)]
-        start_all(to_cols, 0, points_own, right_all, cols_n, my_place)
-        start_all(to_rows, 0, first_own, first_all, rows_n, my_slot)
+        for n in range(1, each):
+            to_rows(0, first_own, first_all, n * turns, my_slot).start()
+
+        @pl.when(my_turn == 0)
+        def _():
+            start_all(to_cols, 0, points_own, right_all, cols_n, my_place)
+
+        def send_group(turn):
+            @pl.loop(0, each)
+            def _(n):
+                to_rows(0, first_own, first_all, n * turns + turn, my_slot).start()
+
+        send_group(1)
         first_all[my_slot] = first_own[...]
         right_all[my_place] = z_own
 
@@ -178,6 +191,8 @@
                 vec_own[call] = block
                 vec_all[call, my_slot] = block
                 start_all(to_rows, 1 + call, vec_own.at[call], vec_all.at[call], rows_n, my_slot)
+                col_all[call, my_place] = block
+                start_all(to_cols, 6 + call, vec_own.at[call], col_all.at[call], cols_n, my_place)
 
         def take_piece(call, piece):
             for n in range(2):
@@ -194,34 +209,43 @@
                 right[:, pl.ds(pl.multiple_of(place * own, 128), own)] = stacked(right_all[place], False).astype(BF16)
             acc_ref[0] = jnp.zeros((4 * VECS, CHUNK), F32)
 
-            @pl.loop(0, n_pieces)
+            @pl.loop(0, turns)
             def _(turn):
-                piece = lax.rem(my_slot // 2 + turn, n_pieces)
+                group = lax.rem(my_turn + turn, turns)
 
                 @pl.when(chunk == 0)
                 def _():
-                    for n in range(2):
-                        slot = piece * 2 + n
+                    for n in range(each):
+                        slot = group * each + n
                         arrived(to_rows, 0, first_own, first_all, slot, my_slot)
                         here = pl.ds(pl.multiple_of(slot * own, 128), own)
                         left[here, :] = stacked(first_all[slot, 0:VECS], True).T.astype(BF16)
                         put_vecs(slot, first_all[slot, VECS:])
 
-                count = chunk * n_pieces + turn
-                slot = lax.rem(count, STAGES)
-
-                @pl.when(count >= STAGES)
-                def _():
-                    pltpu.make_async_copy(stage.at[slot], low.at[0], stage_sem.at[slot]).wait()
+                    @pl.when(turn + 2 < turns)
+                    def _():
+                        send_group(turn + 2)
+
+                    @pl.when((turn == 0) & (my_turn != 0))
+                    def _():
+                        start_all(to_cols, 0, points_own, right_all, cols_n, my_place)
+
+                count = chunk * turns + turn
+                half = pl.ds(pl.multiple_of(lax.rem(count, 2) * GROUP, GROUP), GROUP)
+                sem = stage_sem.at[lax.rem(count, 2)]
+
+                @pl.when(count >= 2)
+                def _():
+                    pltpu.make_async_copy(stage.at[half], low.at[0], sem).wait()
 
                 acc = acc_low = None
-                for sub in range(PIECE // SUB):
-                    rows = pl.ds(pl.multiple_of(piece * PIECE + sub * SUB, SUB), SUB)
+                for sub in range(GROUP // SUB):
+                    rows = pl.ds(pl.multiple_of(group * GROUP + sub * SUB, SUB), SUB)
                     m = matern(jnp.dot(left[rows, :], right[:, cols], preferred_element_type=F32))
                     h = m.astype(BF16)
                     l = (m - h.astype(F32)).astype(BF16)
                     high[rows, cols] = h
-                    stage[slot, sub * SUB:(sub + 1) * SUB, :] = l
+                    stage[pl.ds(pl.multiple_of(lax.rem(count, 2) * GROUP + sub * SUB, SUB), SUB), :] = l
                     more = jnp.dot(vecs[:, rows], h, preferred_element_type=F32)
                     more_low = jnp.dot(vecs[0:VECS, rows], l, preferred_element_type=F32)
                     acc = more if acc is None else acc + more
@@ -229,17 +253,15 @@
                 acc_ref[0, 0:3 * VECS] += acc
                 acc_ref[0, 3 * VECS:] += acc_low
 
-                kept = is_kept(piece, chunk)
+                kept = is_kept(group, chunk)
 
                 @pl.when(kept)
                 def _():
-                    pltpu.make_async_copy(
-                        stage.at[slot], low.at[kept_at(piece, chunk)], stage_sem.at[slot]
-                    ).start()
+                    pltpu.make_async_copy(stage.at[half], low.at[chunk], sem).start()
 
                 @pl.when(jnp.logical_not(kept))
                 def _():
-                    pltpu.make_async_copy(stage.at[slot], low_hbm.at[chunk, piece], stage_sem.at[slot]).start()
+                    pltpu.make_async_copy(stage.at[half], low_hbm.at[chunk, group], sem).start()
 
             send_part(0, chunk, acc_ref[0])
             for turn in range(n_chunks - 1):
@@ -247,18 +269,19 @@
                 def _():
                     owner_step(0, turn)
 
-        for slot in range(STAGES):
-            pltpu.make_async_copy(stage.at[slot], low.at[0], stage_sem.at[slot]).wait()
+        for n in range(2):
+            pltpu.make_async_copy(stage.at[pl.ds(n * GROUP, GROUP)], low.at[0], stage_sem.at[n]).wait()
 
         early = [(piece, chunk) for piece in range(EARLY) for chunk in range(n_chunks)]
         late = [(piece, chunk) for chunk in range(n_chunks) for piece in range(EARLY, n_pieces)]
         units = early + late
-        far = [unit for unit in units if not is_kept(*unit)]
+        far = [(piece, chunk) for piece, chunk in units if not is_kept(piece // 2, chunk)]
 
         def fetch(count):
             piece, chunk = far[count % len(far)]
             slot = count % STAGES
-            return pltpu.make_async_copy(low_hbm.at[chunk, piece], stage.at[slot], stage_sem.at[slot])
+            away = low_hbm.at[chunk, piece // 2, pl.ds(piece % 2 * PIECE, PIECE)]
+            return pltpu.make_async_copy(away, stage.at[pl.ds(slot * PIECE, PIECE)], stage_sem.at[slot])
 
         def product(call, fetched, last, hooks):
             for number, (piece, chunk) in enumerate(units):
@@ -269,13 +292,13 @@
                 rows = slice(piece * PIECE, (piece + 1) * PIECE)
                 cols = slice(chunk * CHUNK, (chunk + 1) * CHUNK)
                 acc = jnp.dot(vecs[:, rows], high[rows, cols], preferred_element_type=F32)
-                if is_kept(piece, chunk):
-                    below = low[kept_at(piece, chunk)]
+                if is_kept(piece // 2, chunk):
+                    below = low[chunk, piece % 2 * PIECE:(piece % 2 + 1) * PIECE]
                 else:
                     fetch(fetched).wait()
-                    below = stage[fetched % STAGES]
+                    below = stage[fetched % STAGES * PIECE:(fetched % STAGES + 1) * PIECE]
                 acc_low = jnp.dot(vecs[0:VECS, rows], below, preferred_element_type=F32)
-                if not is_kept(piece, chunk):
+                if not is_kept(piece // 2, chunk):
                     if not (last and fetched + STAGES >= 2 * len(far)):
                         fetch(fetched + STAGES).start()
                     fetched += 1
@@ -292,16 +315,18 @@
         row_of = lax.broadcasted_iota(jnp.int32, (VECS, 128), 0)
         lane_of = lax.broadcasted_iota(jnp.int32, (VECS, 128), 1)
 
-        def dots_local(phase, pairs):
+        def dots_local(phase, values):
             line = jnp.zeros((1, 128), F32)
-            for n, (x, y) in enumerate(pairs):
-                value = jnp.sum(x * y, axis=1, keepdims=True)
+            for n, value in enumerate(values):
                 here = lane_of == row_of + n * VECS
                 line = line + jnp.sum(jnp.where(here, value, 0.0), axis=0, keepdims=True)
             block = jnp.broadcast_to(line, (8, 128))
             dot_a[phase] = block
             dot_a_all[phase, my_col] = block
             start_all(to_cols, 4 + phase, dot_a.at[phase], dot_a_all.at[phase], cols_n, my_col)
+
+        def dot(x, y):
+            return jnp.sum(x * y, axis=1, keepdims=True)
 
         def dots_row(phase):
             @pl.loop(1, cols_n)
@@ -335,6 +360,9 @@
             for call in range(2):
                 sent_parts(call)
                 sent_all(to_rows, 1 + call, vec_own.at[call], vec_all.at[call], rows_n)
+                sent_all(to_cols, 6 + call, vec_own.at[call], col_all.at[call], cols_n)
+                for place in range(cols_n):
+                    arrived(to_cols, 6 + call, vec_own.at[call], col_all.at[call], place, my_place)
 
         def sent_parts(call):
             @pl.loop(1, cols_n)
@@ -373,7 +401,7 @@
         fetched = product(2, fetched, True, merged(
             hooks_after(1),
             {
-                14: [lambda: dots_local(0, [(vec_own[0], vec_own[0]), (vec_own[0], vec_own[1])])],
+                14: [lambda: dots_local(0, [dot(vec_own[0], vec_own[0]), dot(vec_own[0], vec_own[1])])],
                 18: [sent_before],
                 26: [lambda: dots_row(0)],
             },
@@ -382,16 +410,24 @@
         norm0, curve0 = dots_whole(0, 2)
         alpha0 = norm0 / curve0
         res1 = res0 - alpha0 * image0
+        crossed = jnp.zeros((VECS, own), F32)
+        for place in range(cols_n):
+            owner = lax.rem(first_turn + place // pair, turns) * pair + place % pair
+            there = col_all[0, place] - alpha0 * col_all[1, place]
+            crossed = crossed + there * part[2, owner]
+        dots_local(1, [dot(res1, res1), dot(res1, image0), jnp.sum(crossed, axis=1, keepdims=True)])
+        dots_row(1)
         image1 = reduced(2, image0)
         half = image0 - alpha0 * image1
-        dots_local(1, [(res1, res1), (res1, half), (res1 + res1, image0)])
-        dots_row(1)
-        norm1, own_curve, cross = dots_whole(1, 3)
+        norm1, cross, crossed = dots_whole(1, 3)
+        own_curve = cross - alpha0 * (crossed + NOISE_VAR * cross)
         beta0 = norm1 / norm0
-        curve1 = own_curve + beta0 * cross + beta0 * beta0 * curve0
+        curve1 = own_curve + 2.0 * beta0 * cross + beta0 * beta0 * curve0
         alpha1 = norm1 / curve1
-        sol_ref[...] = init_ref[...] + alpha0 * res0 + alpha1 * (res1 + beta0 * res0)
-        res_ref[...] = res1 - alpha1 * (half + beta0 * image0)
+        out_ref[0] = init_ref[...] + alpha0 * res0
+        out_ref[1] = alpha1 * (res1 + beta0 * res0)
+        out_ref[2] = res1
+        out_ref[3] = -alpha1 * (half + beta0 * image0)
         sent_parts(2)
         for phase in range(2):
             sent_all(to_cols, 4 + phase, dot_a.at[phase], dot_a_all.at[phase], cols_n)
@@ -400,8 +436,8 @@
     def scratch():
         return [
             pltpu.VMEM((span, wide), BF16),
-            pltpu.VMEM((n_chunks * kept_n, PIECE, CHUNK), BF16),
-            pltpu.VMEM((STAGES, PIECE, CHUNK), BF16),
+            pltpu.VMEM((n_chunks, GROUP, CHUNK), BF16),
+            pltpu.VMEM((STAGES * PIECE, CHUNK), BF16),
             pltpu.VMEM((span, DEPTH), BF16),
             pltpu.VMEM((DEPTH, wide), BF16),
             pltpu.VMEM((3 * VECS, span), BF16),
@@ -411,14 +447,15 @@
             pltpu.VMEM((cols_n, VECS, own), F32),
             pltpu.VMEM((2, VECS, own), F32),
             pltpu.VMEM((2, rows_n, VECS, own), F32),
+            pltpu.VMEM((2, cols_n, VECS, own), F32),
             pltpu.VMEM((3, cols_n, VECS, own), F32),
             pltpu.VMEM((3, cols_n, VECS, own), F32),
             pltpu.VMEM((2, 8, 128), F32),
             pltpu.VMEM((2, cols_n, 8, 128), F32),
             pltpu.VMEM((2, 8, 128), F32),
             pltpu.VMEM((2, rows_n, 8, 128), F32),
-            pltpu.SemaphoreType.DMA((6, cols_n)),
-            pltpu.SemaphoreType.DMA((6, cols_n)),
+            pltpu.SemaphoreType.DMA((8, cols_n)),
+            pltpu.SemaphoreType.DMA((8, cols_n)),
             pltpu.SemaphoreType.DMA((5, rows_n)),
             pltpu.SemaphoreType.DMA((5, rows_n)),
             pltpu.SemaphoreType.DMA((STAGES,)),
@@ -428,15 +465,14 @@
     return pl.pallas_call(
         kernel,
         out_shape=[
-            jax.ShapeDtypeStruct((VECS, own), F32),
-            jax.ShapeDtypeStruct((VECS, own), F32),
-            jax.ShapeDtypeStruct((n_chunks, n_pieces, PIECE, CHUNK), BF16),
+            jax.ShapeDtypeStruct((4, VECS, own), F32),
+            jax.ShapeDtypeStruct((n_chunks, turns, GROUP, CHUNK), BF16),
         ],
         in_specs=[vmem] * 4,
-        out_specs=[vmem, vmem, pl.BlockSpec(memory_space=pl.ANY)],
+        out_specs=[vmem, pl.BlockSpec(memory_space=pl.ANY)],
         scratch_shapes=scratch(),
         compiler_params=pltpu.CompilerParams(
-            collective_id=0, has_side_effects=True, vmem_limit_bytes=60 * 2**20
+            collective_id=0, has_side_effects=True, vmem_limit_bytes=63 * 2**20
         ),
         name="conjugate_gradients",
     )
@@ -447,8 +483,8 @@
 
     def shards(points, targets, initial, lengthscale):
         call = make_kernel(rows_n, cols_n, points.shape[0])
-        sol, res, _ = call(points.T, initial.T, targets.T, lengthscale[:, None])
-        return sol.T, res.T
+        out, _ = call(points.T, initial.T, targets.T, lengthscale[None, :])
+        return (out[0] + out[1]).T, (out[2] + out[3]).T
 
     spec = P(("row", "col"), None)
     return jax.shard_map(

time: 135 us -> 119 us (0.88)
  Pallas kernels: 130 us -> 117 us
  local copies, waits for them, and re-layouts: 4.02 us -> 0 us
  other arithmetic: 0 us -> 1.41 us
    pallas_call x1, Pallas kernels: 130 us -> 117 us  [shards(): out, _ = call(points.T, initial.T, targets.T, lengthscale[None, :])]
    unnamed x2 -> x0, local copies, waits for them, and re-layouts: 2.69 us -> none
    transpose x0 -> x1, other arithmetic: none -> 1.41 us  [shards(): return ((out[0] + out[1]).T, (out[2] + out[3]).T)]
where the time goes in v3:
time: 119 us
  Pallas kernels  117 us (98%)
  other arithmetic  1.41 us (1%)
    pallas_call x1, Pallas kernels, shards(): out, _ = call(points.T, initial.T, targets.T, lengthscale[None, :])  117 us

profile of v3, /device:TPU:1, one launch (start us, length us, event | category | flops | bytes accessed | tf_op | source)
XLA Modules:
  0.0 119.2 jit_solution(11157504994259876999)
XLA Ops:
  0.6 117.2 %conjugate_gradients.1 = (f32[4,16,384]{2,1,0:T(8,128)}, bf16[4,4,1536,768]{3,2,1,0:T(8,128)(2,1)}) custom-call(f32[16,384]{1,0:T(8,128)} %bitcast.12, f32[16,384]{1,0:T(8,128)} %bitcast.13, f32[16,384]{1,0:T(8,128)} %bitcast.14, f32[1,16]{1,0:T(1,128)} %bitcast.15), custom_call_target="tpu_custom_call" | custom-call | tf_op jit(solution)/shard_map/conjugate_gradients/pallas_call | solution.py:486
  117.8 1.4 %add_bitcast_fusion = (f32[384,16]{0,1:T(8,128)}, f32[384,16]{0,1:T(8,128)}) fusion(f32[4,16,384]{2,1,0:T(8,128)} %get-tuple-element.3), kind=kLoop, calls=%fused_computation | loop fusion | flops 12288 | bytes 147456 | tf_op jit(solution)/shard_map/transpose | solution.py:487

commit v4 on v3

--- a/solution.py
+++ b/solution.py
@@ -17,7 +17,8 @@
 CHUNK = 768
 PIECE = 768
 GROUP = 2 * PIECE
-SUB = 512
+SUB = 768
+TILE = 256
 STAGES = 4
 EARLY = 3
 LAG = 7
@@ -192,7 +193,9 @@
                 vec_all[call, my_slot] = block
                 start_all(to_rows, 1 + call, vec_own.at[call], vec_all.at[call], rows_n, my_slot)
                 col_all[call, my_place] = block
-                start_all(to_cols, 6 + call, vec_own.at[call], col_all.at[call], cols_n, my_place)
+
+        def spread_cols(call):
+            start_all(to_cols, 6 + call, vec_own.at[call], col_all.at[call], cols_n, my_place)
 
         def take_piece(call, piece):
             for n in range(2):
@@ -202,7 +205,6 @@
 
         @pl.loop(0, n_chunks)
         def _(chunk):
-            cols = pl.ds(pl.multiple_of(chunk * CHUNK, CHUNK), CHUNK)
             for n in range(pair):
                 place = chunk * pair + n
                 arrived(to_cols, 0, points_own, right_all, place, my_place)
@@ -238,20 +240,18 @@
                 def _():
                     pltpu.make_async_copy(stage.at[half], low.at[0], sem).wait()
 
-                acc = acc_low = None
                 for sub in range(GROUP // SUB):
                     rows = pl.ds(pl.multiple_of(group * GROUP + sub * SUB, SUB), SUB)
-                    m = matern(jnp.dot(left[rows, :], right[:, cols], preferred_element_type=F32))
-                    h = m.astype(BF16)
-                    l = (m - h.astype(F32)).astype(BF16)
-                    high[rows, cols] = h
-                    stage[pl.ds(pl.multiple_of(lax.rem(count, 2) * GROUP + sub * SUB, SUB), SUB), :] = l
-                    more = jnp.dot(vecs[:, rows], h, preferred_element_type=F32)
-                    more_low = jnp.dot(vecs[0:VECS, rows], l, preferred_element_type=F32)
-                    acc = more if acc is None else acc + more
-                    acc_low = more_low if acc_low is None else acc_low + more_low
-                acc_ref[0, 0:3 * VECS] += acc
-                acc_ref[0, 3 * VECS:] += acc_low
+                    staged = pl.ds(pl.multiple_of(lax.rem(count, 2) * GROUP + sub * SUB, SUB), SUB)
+                    for n in range(0, CHUNK, TILE):
+                        here = pl.ds(pl.multiple_of(chunk * CHUNK + n, TILE), TILE)
+                        m = matern(jnp.dot(left[rows, :], right[:, here], preferred_element_type=F32))
+                        h = m.astype(BF16)
+                        l = (m - h.astype(F32)).astype(BF16)
+                        high[rows, here] = h
+                        stage[staged, n:n + TILE] = l
+                        acc_ref[0, 0:3 * VECS, n:n + TILE] += jnp.dot(vecs[:, rows], h, preferred_element_type=F32)
+                        acc_ref[0, 3 * VECS:, n:n + TILE] += jnp.dot(vecs[0:VECS, rows], l, preferred_element_type=F32)
 
                 kept = is_kept(group, chunk)
 
@@ -397,13 +397,14 @@
 
         for count in range(STAGES):
             fetch(count).start()
-        fetched = product(1, 0, False, merged(hooks_after(0), hooks_within(1)))
+        fetched = product(1, 0, False, merged(hooks_after(0), hooks_within(1), {20: [lambda: spread_cols(0)]}))
         fetched = product(2, fetched, True, merged(
             hooks_after(1),
             {
+                12: [lambda: spread_cols(1)],
                 14: [lambda: dots_local(0, [dot(vec_own[0], vec_own[0]), dot(vec_own[0], vec_own[1])])],
-                18: [sent_before],
-                26: [lambda: dots_row(0)],
+                24: [lambda: dots_row(0)],
+                28: [sent_before],
             },
         ))
         res0, image0 = vec_own[0], vec_own[1]

time: 119 us -> 116 us (0.975)
  Pallas kernels: 117 us -> 113 us
    pallas_call x1, Pallas kernels: 117 us -> 113 us  [shards(): out, _ = call(points.T, initial.T, targets.T, lengthscale[None, :])]
where the time goes in v4:
time: 116 us; the launch traced here: 115 us
  Pallas kernels  113 us (97%)
  other arithmetic  1.41 us (1%)
    pallas_call x1, Pallas kernels, shards(): out, _ = call(points.T, initial.T, targets.T, lengthscale[None, :])  113 us

profile of v4, /device:TPU:1, one launch (start us, length us, event | category | flops | bytes accessed | tf_op | source)
XLA Modules:
  0.0 115.3 jit_solution(6297736998478590535)
XLA Ops:
  0.6 113.2 %conjugate_gradients.1 = (f32[4,16,384]{2,1,0:T(8,128)}, bf16[4,4,1536,768]{3,2,1,0:T(8,128)(2,1)}) custom-call(f32[16,384]{1,0:T(8,128)} %bitcast.12, f32[16,384]{1,0:T(8,128)} %bitcast.13, f32[16,384]{1,0:T(8,128)} %bitcast.14, f32[1,16]{1,0:T(1,128)} %bitcast.15), custom_call_target="tpu_custom_call" | custom-call | tf_op jit(solution)/shard_map/conjugate_gradients/pallas_call | solution.py:487
  113.9 1.4 %add_bitcast_fusion = (f32[384,16]{0,1:T(8,128)}, f32[384,16]{0,1:T(8,128)}) fusion(f32[4,16,384]{2,1,0:T(8,128)} %get-tuple-element.3), kind=kLoop, calls=%fused_computation | loop fusion | flops 12288 | bytes 147456 | tf_op jit(solution)/shard_map/transpose | solution.py:488

commit v5 on v4

--- a/solution.py
+++ b/solution.py
@@ -21,7 +21,7 @@
 TILE = 256
 STAGES = 4
 EARLY = 3
-LAG = 7
+LAG = 6
 
 
 def split3(x):
@@ -108,14 +108,14 @@
         def to_rows(phase, src, dst, k, slot):
             return pltpu.make_async_remote_copy(
                 src_ref=src, dst_ref=dst.at[slot],
-                send_sem=row_send.at[phase, k], recv_sem=row_recv.at[phase, slot],
+                send_sem=row_send.at[phase], recv_sem=row_recv.at[phase, slot],
                 device_id=(lax.rem(my_row + k, rows_n), my_col), device_id_type=MESH,
             )
 
         def to_cols(phase, src, dst, k, slot):
             return pltpu.make_async_remote_copy(
                 src_ref=src, dst_ref=dst.at[slot],
-                send_sem=col_send.at[phase, k], recv_sem=col_recv.at[phase, slot],
+                send_sem=col_send.at[phase], recv_sem=col_recv.at[phase, slot],
                 device_id=(my_row, lax.rem(my_col + k, cols_n)), device_id_type=MESH,
             )
 
@@ -124,10 +124,9 @@
             def _(k):
                 make(phase, src, dst, k, slot).start()
 
-        def sent_all(make, phase, src, dst, count):
-            @pl.loop(1, count)
-            def _(k):
-                make(phase, src, dst, k, 0).wait_send()
+        def sent_all(sems, phase, dst, count):
+            bulk = dst.at[pl.ds(0, count - 1)]
+            pltpu.make_async_copy(bulk, bulk, sems.at[phase]).wait()
 
         def arrived(make, phase, src, dst, slot, mine):
             @pl.when(slot != mine)
@@ -320,9 +319,8 @@
             for n, value in enumerate(values):
                 here = lane_of == row_of + n * VECS
                 line = line + jnp.sum(jnp.where(here, value, 0.0), axis=0, keepdims=True)
-            block = jnp.broadcast_to(line, (8, 128))
-            dot_a[phase] = block
-            dot_a_all[phase, my_col] = block
+            dot_a[phase] = line
+            dot_a_all[phase, my_col] = line
             start_all(to_cols, 4 + phase, dot_a.at[phase], dot_a_all.at[phase], cols_n, my_col)
 
         def dot(x, y):
@@ -348,26 +346,24 @@
             total = dot_b_all[phase, 0]
             for slot in range(1, rows_n):
                 total = total + dot_b_all[phase, slot]
-            line = jnp.broadcast_to(total[0:1], (VECS, 128))
+            line = jnp.broadcast_to(total, (VECS, 128))
             return [
                 jnp.sum(jnp.where(lane_of == row_of + n * VECS, line, 0.0), axis=1, keepdims=True)
                 for n in range(count)
             ]
 
         def sent_before():
-            sent_all(to_cols, 0, points_own, right_all, cols_n)
-            sent_all(to_rows, 0, first_own, first_all, rows_n)
+            sent_all(col_send, 0, right_all, cols_n)
+            sent_all(row_send, 0, first_all, rows_n)
             for call in range(2):
                 sent_parts(call)
-                sent_all(to_rows, 1 + call, vec_own.at[call], vec_all.at[call], rows_n)
-                sent_all(to_cols, 6 + call, vec_own.at[call], col_all.at[call], cols_n)
+                sent_all(row_send, 1 + call, vec_all.at[call], rows_n)
+                sent_all(col_send, 6 + call, col_all.at[call], cols_n)
                 for place in range(cols_n):
                     arrived(to_cols, 6 + call, vec_own.at[call], col_all.at[call], place, my_place)
 
         def sent_parts(call):
-            @pl.loop(1, cols_n)
-            def _(k):
-                part_copy(call, lax.rem(my_col + k, cols_n), 0).wait_send()
+            sent_all(col_send, 1 + call, part_all.at[call], cols_n)
 
         def hooks_after(call):
             found = {}
@@ -431,8 +427,8 @@
         out_ref[3] = -alpha1 * (half + beta0 * image0)
         sent_parts(2)
         for phase in range(2):
-            sent_all(to_cols, 4 + phase, dot_a.at[phase], dot_a_all.at[phase], cols_n)
-            sent_all(to_rows, 3 + phase, dot_b.at[phase], dot_b_all.at[phase], rows_n)
+            sent_all(col_send, 4 + phase, dot_a_all.at[phase], cols_n)
+            sent_all(row_send, 3 + phase, dot_b_all.at[phase], rows_n)
 
     def scratch():
         return [
@@ -451,13 +447,13 @@
             pltpu.VMEM((2, cols_n, VECS, own), F32),
             pltpu.VMEM((3, cols_n, VECS, own), F32),
             pltpu.VMEM((3, cols_n, VECS, own), F32),
-            pltpu.VMEM((2, 8, 128), F32),
-            pltpu.VMEM((2, cols_n, 8, 128), F32),
-            pltpu.VMEM((2, 8, 128), F32),
-            pltpu.VMEM((2, rows_n, 8, 128), F32),
+            pltpu.VMEM((2, 1, 128), F32),
+            pltpu.VMEM((2, cols_n, 1, 128), F32),
+            pltpu.VMEM((2, 1, 128), F32),
+            pltpu.VMEM((2, rows_n, 1, 128), F32),
+            pltpu.SemaphoreType.DMA((8,)),
             pltpu.SemaphoreType.DMA((8, cols_n)),
-            pltpu.SemaphoreType.DMA((8, cols_n)),
-            pltpu.SemaphoreType.DMA((5, rows_n)),
+            pltpu.SemaphoreType.DMA((5,)),
             pltpu.SemaphoreType.DMA((5, rows_n)),
             pltpu.SemaphoreType.DMA((STAGES,)),
         ]

time: 116 us -> 113 us (0.974)
  Pallas kernels: 113 us -> 111 us
    pallas_call x1, Pallas kernels: 113 us -> 111 us  [shards(): out, _ = call(points.T, initial.T, targets.T, lengthscale[None, :])]
where the time goes in v5:
time: 113 us
  Pallas kernels  111 us (98%)
  other arithmetic  1.41 us (1%)
    pallas_call x1, Pallas kernels, shards(): out, _ = call(points.T, initial.T, targets.T, lengthscale[None, :])  111 us

profile of v5, /device:TPU:1, one launch (start us, length us, event | category | flops | bytes accessed | tf_op | source)
XLA Modules:
  0.0 112.8 jit_solution(9714775275457226449)
XLA Ops:
  0.6 110.8 %conjugate_gradients.1 = (f32[4,16,384]{2,1,0:T(8,128)}, bf16[4,4,1536,768]{3,2,1,0:T(8,128)(2,1)}) custom-call(f32[16,384]{1,0:T(8,128)} %bitcast.12, f32[16,384]{1,0:T(8,128)} %bitcast.13, f32[16,384]{1,0:T(8,128)} %bitcast.14, f32[1,16]{1,0:T(1,128)} %bitcast.15), custom_call_target="tpu_custom_call" | custom-call | tf_op jit(solution)/shard_map/conjugate_gradients/pallas_call | solution.py:483
  111.4 1.4 %add_bitcast_fusion = (f32[384,16]{0,1:T(8,128)}, f32[384,16]{0,1:T(8,128)}) fusion(f32[4,16,384]{2,1,0:T(8,128)} %get-tuple-element.3), kind=kLoop, calls=%fused_computation | loop fusion | flops 12288 | bytes 147456 | tf_op jit(solution)/shard_map/transpose | solution.py:484
